TPU v7x, 32 devices: a whole 2x2x4 slice. The times are simulated.
32 devices in a mesh: ccd: 4 (over y, core), tile: 8 (over z, x).
Axes of the slice: x: 2, y: 2, z: 4, core: 2. Of those that a mesh axis runs over, the one named last changes fastest.
Arguments:
- exposures: float32 [8, 2048, 4096], P('tile', 'ccd'), may hold values from -6 to 6
- interp: bfloat16 [8, 32, 256, 128], P('tile'), may hold values from -0.375 to 0.375
- col_offsets: int32 [8, 32], P('tile'), may hold values from 0 to 30
- template: float32 [2048, 4096], P('ccd', 'tile'), may hold values from -6 to 6
- coef_table: float32 [8, 4, 3, 3], replicated, may hold values from -3 to 3
- coef_index: int32 [8, 4, 8], replicated, may hold values from 0 to 3
- intersection: int32 [8, 4, 8], replicated, may hold values 0 or 1
Outputs:
- difference: float32 [8, 2048, 4096], P('tile', 'ccd')
All inputs are finite; a program needn't handle non-finite values.
Results may differ from a plain program's by a relative error of at most 0.0029.
Values sent between devices are 32-bit elements; how exact they have to be, the bound alone decides.
A program may use at most 128 MiB of HBM per device.

v0:
```python
import jax
import jax.numpy as jnp
from jax import lax
from jax.sharding import PartitionSpec as P

HALF = 10
KSETS = 4
SIGMAS = (1.5, 3.0, 5.0)


def extended(array, sides, width):
    for axis, dim in sides:
        size, length = (lax.axis_size(axis), array.shape[dim])
        up = [(i, (i + 1) % size) for i in range(size - 1)]
        down = [(j, i) for i, j in up]
        last = lax.slice_in_dim(array, length - width, length, axis=dim)
        leading = lax.slice_in_dim(array, 0, width, axis=dim)
        before = lax.ppermute(last, axis, up)
        after = lax.ppermute(leading, axis, down)
        array = jnp.concatenate([before, array, after], axis=dim)
    return array


def basis_taps(half_width):
    positions = jnp.arange(-half_width, half_width + 1).astype(jnp.float32)
    kernels = []
    for sigma_value in SIGMAS:
        gauss = jnp.exp(-0.5 * (positions / sigma_value) ** 2)
        kernels.append(gauss / jnp.sum(gauss))
    return kernels


def smooth(padded, gauss, out_rows, out_cols):
    tap_count = gauss.shape[0]
    across = gauss[0] * padded[0:out_rows, :]
    for offset in range(1, tap_count):
        across = across + gauss[offset] * padded[offset : offset + out_rows, :]
    result = gauss[0] * across[:, 0:out_cols]
    for offset in range(1, tap_count):
        result = result + gauss[offset] * across[:, offset : offset + out_cols]
    return result


def resample(exposure_img, weights, offsets):
    row_count = exposure_img.shape[0]
    block_count = weights.shape[0]
    block_cols = weights.shape[2]
    tiles = exposure_img.astype(jnp.bfloat16).reshape(row_count, block_count, block_cols)
    first_part = jnp.take(tiles, offsets, axis=1)
    second_part = jnp.take(tiles, offsets + 1, axis=1)
    window = jnp.concatenate([first_part, second_part], axis=2)
    output = jnp.einsum("rjk,jkn->rjn", window, weights, preferred_element_type=jnp.float32)
    return output.reshape(row_count, block_count * block_cols)


def on_device(exposures, interp, col_offsets, template, coef_table, coef_index, intersection):
    row_count = exposures.shape[1]
    col_count = exposures.shape[2]
    patch_cols = template.shape[1]
    kernels = basis_taps(HALF)
    patch_row = lax.axis_index("ccd")
    my_epoch = lax.axis_index("tile")
    warped = resample(exposures[0], interp[0], col_offsets[0])
    row_coord = (jnp.arange(row_count).astype(jnp.float32) - (row_count - 1) / 2.0) / (
        row_count / 2.0
    )
    set_range = jnp.arange(KSETS)
    padded = extended(template, (("ccd", 0), ("tile", 1)), HALF)
    smoothed = [smooth(padded, gauss, row_count, patch_cols) for gauss in kernels]
    row_bases = (
        lax.all_gather(smoothed[0], "tile", axis=1, tiled=True),
        lax.all_gather(smoothed[1], "tile", axis=1, tiled=True),
        lax.all_gather(smoothed[2], "tile", axis=1, tiled=True),
    )
    set_ids = coef_index[my_epoch, patch_row]
    set_pick = (set_ids[:, None] == set_range[None, :]).astype(jnp.float32)
    kernel_coef = jnp.sum(set_pick[:, :, None, None] * coef_table[my_epoch][None], axis=1)
    column_coef = jnp.repeat(kernel_coef, patch_cols, axis=0)
    col_coord = (
        (jnp.arange(col_count) % patch_cols).astype(jnp.float32) - (patch_cols - 1) / 2.0
    ) / (patch_cols / 2.0)
    template_model = None
    for kernel_index in range(3):
        const_part = column_coef[:, kernel_index, 0][None, :]
        col_slope = column_coef[:, kernel_index, 1][None, :]
        row_slope = column_coef[:, kernel_index, 2][None, :]
        weight_map = const_part + col_slope * col_coord[None, :] + row_slope * row_coord[:, None]
        contrib = weight_map * row_bases[kernel_index]
        template_model = contrib if template_model is None else template_model + contrib
    coverage = jnp.repeat(intersection[my_epoch, patch_row].astype(jnp.float32), patch_cols)
    difference = (warped - template_model) * coverage[None, :]
    return difference[None]


def solution(mesh):
    placed = (
        P("tile", "ccd", None),
        P("tile", None, None, None),
        P("tile", None),
        P("ccd", "tile"),
        P(),
        P(),
        P(),
    )
    return jax.shard_map(
        on_device, mesh=mesh, in_specs=placed, out_specs=P("tile", "ccd", None), check_vma=False
    )
```

profile of v0, /device:TPU:0, one launch (start us, length us, event | category | flops | bytes accessed | tf_op | source)
XLA Modules:
  0.0 469.4 jit_solution(13398346818644322910)
XLA Ops:
  6.5 0.9 fusion.79
  7.5 1.4 collective-permute-start.1
  8.9 3.0 collective-permute-start
  12.6 0.7 broadcast_divide_fusion
  13.2 0.7 fusion.85
  14.0 1.2 pad_maximum_fusion.3
  15.1 1.3 collective-permute-start.3
  16.4 5.5 %collective-permute-start.2 = (f32[532,10]{1,0:T(8,128)S(1)}, f32[532,10]{1,0:T(8,128)S(1)}, u32[]{:S(2)}, u32[]{:S(2)}) collective-permute-start(f32[532,10]{1,0:T(8,128)S(1)} %get-tuple-element.8), channel_id=1, source_target_pairs={{0,1},{1,2},{2,3},{3,4},{4,5},{5,6},{6,7},{8,9},{9,10},{10,11},{11... | collective-permute-start | bytes 63848 | tf_op jit(solution)/shard_map/ppermute | solution.py:18
  22.6 4.2 collective-permute-done.3
  26.8 6.9 %collective-permute-done.2 = f32[532,10]{1,0:T(8,128)S(1)} collective-permute-done((f32[532,10]{1,0:T(8,128)S(1)}, f32[532,10]{1,0:T(8,128)S(1)}, u32[]{:S(2)}, u32[]{:S(2)}) %collective-permute-start.2) | collective-permute-done | bytes 21312 | tf_op jit(solution)/shard_map/ppermute | solution.py:18
  34.2 16.5 %multiply_add_fusion = f32[512,532]{1,0:T(8,128)S(1)} fusion(f32[532,532]{1,0:T(8,128)S(1)} %pad_maximum_fusion, f32[]{:T(128)} %bitcast.81, f32[]{:T(128)} %bitcast.80, f32[]{:T(128)} %bitcast.79, f32[]{:T(128)} %bitcast.78, f32[]{:T(128)} %bitcast.77, f32[]{:T(128)} %bitcast.76, f32[]{:T(128)} %bitcast.75, f32[]{:T(128)} %bitcast.74, f32[]{:T(128)} %bitcast.73, ...), kind=kLoop, calls=%fused_computation.11 | loop fusion | flops 11167744 | bytes 23969876 | tf_op jit(solution)/shard_map/add | solution.py:37
  50.7 19.6 %fusion.5 = f32[512,512]{1,0:T(8,128)} fusion(f32[512,532]{1,0:T(8,128)S(1)} %multiply_add_fusion, f32[]{:T(128)} %bitcast.81, f32[]{:T(128)} %bitcast.80, f32[]{:T(128)} %bitcast.79, f32[]{:T(128)} %bitcast.78, f32[]{:T(128)} %bitcast.77, f32[]{:T(128)} %bitcast.76, f32[]{:T(128)} %bitcast.75, f32[]{:T(128)} %bitcast.74, f32[]{:T(128)} %bitcast.73, ...), kind=kLoop, calls=%fused_computation.15 | loop fusion | flops 10747904 | bytes 23068756 | tf_op jit(solution)/shard_map/add | solution.py:40
  71.0 0.7 broadcast_divide_fusion.1
  72.3 0.7 fusion.83
  73.0 16.3 %multiply_add_fusion.1 = f32[512,532]{1,0:T(8,128)S(1)} fusion(f32[532,532]{1,0:T(8,128)S(1)} %pad_maximum_fusion, f32[]{:T(128)} %bitcast.57, f32[]{:T(128)} %bitcast.56, f32[]{:T(128)} %bitcast.55, f32[]{:T(128)} %bitcast.54, f32[]{:T(128)} %bitcast.53, f32[]{:T(128)} %bitcast.52, f32[]{:T(128)} %bitcast.51, f32[]{:T(128)} %bitcast.50, f32[]{:T(128)} %bitcast.49, ...), kind=kLoop, calls=%fused_computation.12 | loop fusion | flops 11167744 | bytes 23969876 | tf_op jit(solution)/shard_map/add | solution.py:37
  89.3 19.3 %fusion.25 = f32[512,512]{1,0:T(8,128)} fusion(f32[512,532]{1,0:T(8,128)S(1)} %multiply_add_fusion.1, f32[]{:T(128)} %bitcast.57, f32[]{:T(128)} %bitcast.56, f32[]{:T(128)} %bitcast.55, f32[]{:T(128)} %bitcast.54, f32[]{:T(128)} %bitcast.53, f32[]{:T(128)} %bitcast.52, f32[]{:T(128)} %bitcast.51, f32[]{:T(128)} %bitcast.50, f32[]{:T(128)} %bitcast.49, ...), kind=kLoop, calls=%fused_computation.56 | loop fusion | flops 10747904 | bytes 23068756 | tf_op jit(solution)/shard_map/add | solution.py:40
  109.4 0.7 broadcast_divide_fusion.2
  110.1 0.7 fusion.82
  110.7 0.7 fusion.81
  111.5 16.5 %multiply_add_fusion.2 = f32[512,532]{1,0:T(8,128)S(1)} fusion(f32[532,532]{1,0:T(8,128)S(1)} %pad_maximum_fusion, f32[]{:T(128)} %bitcast.33, f32[]{:T(128)} %bitcast.32, f32[]{:T(128)} %bitcast.31, f32[]{:T(128)} %bitcast.30, f32[]{:T(128)} %bitcast.29, f32[]{:T(128)} %bitcast.28, f32[]{:T(128)} %bitcast.27, f32[]{:T(128)} %bitcast.26, f32[]{:T(128)} %bitcast.25, ...), kind=kLoop, calls=%fused_computation.13 | loop fusion | flops 11167744 | bytes 23969876 | tf_op jit(solution)/shard_map/add | solution.py:37
  128.0 19.6 %fusion.45 = f32[512,512]{1,0:T(8,128)} fusion(f32[512,532]{1,0:T(8,128)S(1)} %multiply_add_fusion.2, f32[]{:T(128)} %bitcast.33, f32[]{:T(128)} %bitcast.32, f32[]{:T(128)} %bitcast.31, f32[]{:T(128)} %bitcast.30, f32[]{:T(128)} %bitcast.29, f32[]{:T(128)} %bitcast.28, f32[]{:T(128)} %bitcast.27, f32[]{:T(128)} %bitcast.26, f32[]{:T(128)} %bitcast.25, ...), kind=kLoop, calls=%fused_computation.97 | loop fusion | flops 10747904 | bytes 23068756 | tf_op jit(solution)/shard_map/add | solution.py:40
  147.6 7.3 %copy.23 = bf16[1,512,4096]{1,2,0:T(8,128)(2,1)} copy(f32[1,512,4096]{2,1,0:T(8,128)} %param.9) | data formatting | bytes 12582912 | tf_op args[0]
  154.9 6.4 %copy.24 = bf16[512,32,128]{2,0,1:T(8,128)(2,1)} copy(bf16[512,32,128]{0,2,1:T(8,128)(2,1)} %bitcast.108) | data formatting | bytes 8388608 | tf_op jit(solution)/shard_map/convert_element_type | solution.py:48
  161.3 5.3 %gather_fusion.1 = bf16[32,512,128]{2,1,0:T(8,128)(2,1)} fusion(bf16[512,32,128]{2,0,1:T(8,128)(2,1)} %copy.24, s32[1024]{0:T(1024)S(1)} %pad_clamp_fusion), kind=kCustom, calls=%fused_computation.1.clone | custom fusion | bytes 8388736 | tf_op jit(solution)/shard_map/jit(_take)/gather | solution.py:50
  166.6 5.2 %gather_fusion = bf16[32,512,128]{2,1,0:T(8,128)(2,1)} fusion(bf16[512,32,128]{2,0,1:T(8,128)(2,1)} %copy.24, s32[1024]{0:T(1024)S(1)} %pad_clamp_fusion.1), kind=kCustom, calls=%fused_computation.clone | custom fusion | bytes 8388736 | tf_op jit(solution)/shard_map/jit(_take)/gather | solution.py:49
  171.9 5.2 %select_bitcast_fusion = (bf16[512,32,128]{2,0,1:T(8,128)(2,1)S(1)}, bf16[512,32,128]{2,0,1:T(8,128)(2,1)}) fusion(bf16[32,512,128]{2,1,0:T(8,128)(2,1)} %gather_fusion.1, pred[32]{0:T(512)(128)(4,1)S(1)} %get-tuple-element.6, bf16[32,512,128]{2,1,0:T(8,128)(2,1)} %gather_fusion, pred[32]{0:T(512)(128)(4,1)S(1)} %get-tuple-element.84), kind=kLoop, calls=%fused_computation.7 | loop fusion | flops 4194304 | bytes 16777280 | tf_op jit(solution)/shard_map/jit(_take)/select_n | solution.py:50
  177.1 8.5 %fusion = f32[32,512,128]{1,2,0:T(8,128)} fusion(bf16[512,32,128]{2,0,1:T(8,128)(2,1)S(1)} %get-tuple-element.87, bf16[512,32,128]{2,0,1:T(8,128)(2,1)} %get-tuple-element.88, bf16[1,32,256,128]{3,2,1,0:T(8,128)(2,1)S(1)} %copy-done), kind=kOutput, calls=%fused_computation.2 | convolution fusion | flops 1090519040 | bytes 18874368 | tf_op jit(solution)/shard_map/rjk,jkn->rjn/dot_general | solution.py:52
  185.6 8.9 %copy.29 = f32[512,4096]{1,0:T(8,128)} copy(f32[512,4096]{0,1:T(8,128)} %bitcast.107) | data formatting | bytes 16777216 | tf_op jit(solution)/shard_map/reshape | solution.py:53
  194.5 0.7 fusion.72
  196.1 124.9 %all-gather.6.cloned.1.call-done = f32[512,4096]{1,0:T(8,128)} async-done(((f32[512,512]{1,0:T(8,128)}), f32[512,4096]{1,0:T(8,128)}) %all-gather.6.cloned.1.call-update) | async-done | bytes 8388624 | tf_op jit(solution)/shard_map/all_gather | solution.py:72
  321.0 125.3 %all-gather.4.cloned.1.call-done = f32[512,4096]{1,0:T(8,128)} async-done(((f32[512,512]{1,0:T(8,128)}), f32[512,4096]{1,0:T(8,128)}) %all-gather.4.cloned.1.call-update) | async-done | bytes 8388624 | tf_op jit(solution)/shard_map/all_gather | solution.py:71
  446.3 16.6 %multiply_bitcast_fusion = f32[1,512,4096]{2,1,0:T(8,128)} fusion(f32[512,4096]{1,0:T(8,128)} %copy.29, f32[512,4096]{1,0:T(8,128)} %all-gather.8.cloned.1.call-done, f32[512,4096]{1,0:T(8,128)} %all-gather.6.cloned.1.call-done, f32[512,4096]{1,0:T(8,128)} %all-gather.4.cloned.1.call-done, f32[4096]{0:T(1024)S(1)} %bitcast.112, f32[4096]{0:T(1024)S(1)} %bitcast.109, ...), kind=kLoop, calls=%fused_computation.6 | loop fusion | flops 27262976 | bytes 42059776 | tf_op jit(solution)/shard_map/broadcast_in_dim | solution.py:92
  (40 shorter events, 4.8 us)
Async XLA Ops:
  6.5 170.6 %copy-start = (bf16[1,32,256,128]{3,2,1,0:T(8,128)(2,1)S(1)}, bf16[1,32,256,128]{3,2,1,0:T(8,128)(2,1)}, u32[]{:S(2)}) copy-start(bf16[1,32,256,128]{3,2,1,0:T(8,128)(2,1)} %param.10) | copy-start | bytes 6291460
  6.5 189.5 %all-gather.8.cloned.1.call-start = ((), (), s32[]{:S(2)}) async-start(), calls=%async_computation.2 | async-start | bytes 9437184 | tf_op jit(solution)/shard_map/all_gather | solution.py:73
  6.5 27.1 %copy-start.1 = (f32[512,512]{1,0:T(8,128)S(1)}, f32[512,512]{1,0:T(8,128)}, u32[]{:S(2)}) copy-start(f32[512,512]{1,0:T(8,128)} %param.12) | copy-start | bytes 3145732
  7.5 6.5 %collective-permute-start.1 = (f32[10,512]{1,0:T(8,128)S(1)}, f32[10,512]{1,0:T(8,128)S(1)}, u32[]{:S(2)}, u32[]{:S(2)}) collective-permute-start(f32[10,512]{1,0:T(8,128)S(1)} %get-tuple-element.11), channel_id=1, source_target_pairs={{8,0},{16,8},{24,16},{9,1},{17,9},{25,17},{10,2},{18,10},{26,18},{... | collective-permute-start | bytes 61448 | tf_op jit(solution)/shard_map/ppermute | solution.py:19
  8.9 5.1 %collective-permute-start = (f32[10,512]{1,0:T(8,128)S(1)}, f32[10,512]{1,0:T(8,128)S(1)}, u32[]{:S(2)}, u32[]{:S(2)}) collective-permute-start(f32[10,512]{1,0:T(8,128)S(1)} %get-tuple-element.10), channel_id=1, source_target_pairs={{0,8},{8,16},{16,24},{1,9},{9,17},{17,25},{2,10},{10,18},{18,26},{... | collective-permute-start | bytes 61448 | tf_op jit(solution)/shard_map/ppermute | solution.py:18
  15.1 11.6 %collective-permute-start.3 = (f32[532,10]{1,0:T(8,128)S(1)}, f32[532,10]{1,0:T(8,128)S(1)}, u32[]{:S(2)}, u32[]{:S(2)}) collective-permute-start(f32[532,10]{1,0:T(8,128)S(1)} %get-tuple-element.9), channel_id=1, source_target_pairs={{1,0},{2,1},{3,2},{4,3},{5,4},{6,5},{7,6},{9,8},{10,9},{11,10},{12... | collective-permute-start | bytes 63848 | tf_op jit(solution)/shard_map/ppermute | solution.py:19
  16.4 17.2 %collective-permute-start.2 = (f32[532,10]{1,0:T(8,128)S(1)}, f32[532,10]{1,0:T(8,128)S(1)}, u32[]{:S(2)}, u32[]{:S(2)}) collective-permute-start(f32[532,10]{1,0:T(8,128)S(1)} %get-tuple-element.8), channel_id=1, source_target_pairs={{0,1},{1,2},{2,3},{3,4},{4,5},{5,6},{6,7},{8,9},{9,10},{10,11},{11... | collective-permute-start | bytes 63848 | tf_op jit(solution)/shard_map/ppermute | solution.py:18
  70.3 250.6 %all-gather.6.cloned.1.call-start = ((), (), s32[]{:S(2)}) async-start(), calls=%async_computation.1 | async-start | bytes 9437184 | tf_op jit(solution)/shard_map/all_gather | solution.py:72
  108.6 337.7 %all-gather.4.cloned.1.call-start = ((), (), s32[]{:S(2)}) async-start(), calls=%async_computation | async-start | bytes 9437184 | tf_op jit(solution)/shard_map/all_gather | solution.py:71
  154.9 6.4 %copy-start.3 = (s32[1,32]{1,0:T(1,128)S(1)}, s32[1,32]{1,0:T(1,128)}, u32[]{:S(2)}) copy-start(s32[1,32]{1,0:T(1,128)} %param.11) | copy-start | bytes 388
  185.6 9.7 %copy-start.2 = (f32[8,4,3,3]{0,1,3,2:T(4,128)S(1)}, f32[8,4,3,3]{0,1,3,2:T(4,128)}, u32[]{:S(2)}) copy-start(f32[8,4,3,3]{0,1,3,2:T(4,128)} %param.13) | copy-start | bytes 3460
Sparse Core Ops, SparseCore 0:
  70.5 125.1 all-gather.7
  197.8 123.0 all-gather.5
  323.2 123.0 all-gather.3
where the time goes:
time: 471 us; the launch traced here: 469 us
  waiting for transfers between devices  261 us (55%)
  other arithmetic  136 us (29%)
  local copies, waits for them, and re-layouts  38.8 us (8%)
  between operations  13.3 us (3%)
  starting transfers between devices  11.5 us (2%)
  matrix products  8.5 us (2%)
    all_gather x1, waiting for transfers between devices, on_device(): lax.all_gather(smoothed[0], 'tile', axis=1, tiled=True)  125 us
    all_gather x1, waiting for transfers between devices, on_device(): lax.all_gather(smoothed[1], 'tile', axis=1, tiled=True)  125 us
    add x3, other arithmetic, smooth(): result = result + gauss[offset] * across[:, offset:offset + out_cols]  58.4 us
    add x3, other arithmetic, smooth(): across = across + gauss[offset] * padded[offset:offset + out_rows, :]  49.3 us
    broadcast_in_dim x1, other arithmetic, on_device(): return difference[None]  16.6 us
  transfers between devices with their start and end apart: 7, of which 4 were waited for; matrix products, arithmetic and copies ran while one was open for 27% of the time, Pallas kernels for 0%

commit v1 on v0

--- a/solution.py
+++ b/solution.py
@@ -6,6 +6,18 @@
 HALF = 10
 KSETS = 4
 SIGMAS = (1.5, 3.0, 5.0)
+
+
+def collect(value, axis, dim):
+    ways, here, turn = (lax.axis_size(axis), lax.axis_index(axis), value.shape[dim])
+    line, have = (value, 1)
+    while have < ways:
+        line = jnp.concatenate(
+            [line, lax.ppermute(line, axis, [(d, (d - have) % ways) for d in range(ways)])],
+            axis=dim,
+        )
+        have = 2 * have
+    return jnp.roll(line, here * turn, axis=dim)
 
 
 def extended(array, sides, width):
@@ -68,7 +80,7 @@
     padded = extended(template, (("ccd", 0), ("tile", 1)), HALF)
     smoothed = [smooth(padded, gauss, row_count, patch_cols) for gauss in kernels]
     row_bases = (
-        lax.all_gather(smoothed[0], "tile", axis=1, tiled=True),
+        collect(smoothed[0], "tile", 1),
         lax.all_gather(smoothed[1], "tile", axis=1, tiled=True),
         lax.all_gather(smoothed[2], "tile", axis=1, tiled=True),
     )

time: 471 us -> 589 us (1.25)
  waiting for transfers between devices: 261 us -> 338 us
  local copies, waits for them, and re-layouts: 38.8 us -> 61.4 us
  starting transfers between devices: 11.5 us -> 23.3 us
  other arithmetic: 136 us -> 142 us
    ppermute x0 -> x3, waiting for transfers between devices: none -> 328 us  [collect(): lax.ppermute(line, axis, [(d, (d - have) % ways) for d in range(ways)])]
    all_gather x1 -> x0, waiting for transfers between devices: 125 us -> none  [on_device(): lax.all_gather(smoothed[0], 'tile', axis=1, tiled=True)]
    all_gather x1, waiting for transfers between devices: 125 us -> 0.01 us  [on_device(): lax.all_gather(smoothed[1], 'tile', axis=1, tiled=True)]
    unnamed x0 -> x1, other arithmetic: none -> 19.4 us
    add x3 -> x2, other arithmetic: 58.4 us -> 39 us  [smooth(): result = result + gauss[offset] * across[:, offset:offset + out_cols]]
    unnamed x11 -> x21, local copies, waits for them, and re-layouts: 7.4 us -> 23.6 us
    ppermute x0 -> x3, starting transfers between devices: none -> 14.6 us  [collect(): lax.ppermute(line, axis, [(d, (d - have) % ways) for d in range(ways)])]
  transfers between devices with their start and end apart: 7 -> 9, of which waited for: 4 -> 6; matrix products, arithmetic and copies ran while one was open for 27% -> 27% of each run, Pallas kernels for 0% -> 0%
where the time goes in v1:
time: 589 us; the launch traced here: 587 us
  waiting for transfers between devices  338 us (57%)
  other arithmetic  142 us (24%)
  local copies, waits for them, and re-layouts  61.4 us (10%)
  starting transfers between devices  23.3 us (4%)
  between operations  13.5 us (2%)
  matrix products  8.52 us (1%)
    ppermute x3, waiting for transfers between devices, collect(): lax.ppermute(line, axis, [(d, (d - have) % ways) for d in range(ways)])  328 us
    add x3, other arithmetic, smooth(): across = across + gauss[offset] * padded[offset:offset + out_rows, :]  49.3 us
    add x2, other arithmetic, smooth(): result = result + gauss[offset] * across[:, offset:offset + out_cols]  39 us
    unnamed x21, local copies, waits for them, and re-layouts  23.6 us
    unnamed x1, other arithmetic  19.4 us
    broadcast_in_dim x1, other arithmetic, on_device(): return difference[None]  16.6 us
    ppermute x3, starting transfers between devices, collect(): lax.ppermute(line, axis, [(d, (d - have) % ways) for d in range(ways)])  14.6 us
  transfers between devices with their start and end apart: 9, of which 6 were waited for; matrix products, arithmetic and copies ran while one was open for 27% of the time, Pallas kernels for 0%

profile of v1, /device:TPU:0, one launch (start us, length us, event | category | flops | bytes accessed | tf_op | source)
XLA Modules:
  0.0 587.1 jit_solution(6639155434162272977)
XLA Ops:
  7.5 2.5 collective-permute-start
  13.3 1.9 collective-permute-done.1
  16.4 3.4 collective-permute-start.2
  21.7 3.3 collective-permute-done.2
  25.0 4.7 collective-permute-done.3
  30.2 16.5 %multiply_add_fusion.1 = f32[512,532]{1,0:T(8,128)S(1)} fusion(f32[532,532]{1,0:T(8,128)S(1)} %pad_maximum_fusion.2, f32[]{:T(128)} %bitcast.57, f32[]{:T(128)} %bitcast.56, f32[]{:T(128)} %bitcast.55, f32[]{:T(128)} %bitcast.54, f32[]{:T(128)} %bitcast.53, f32[]{:T(128)} %bitcast.52, f32[]{:T(128)} %bitcast.51, f32[]{:T(128)} %bitcast.50, f32[]{:T(128)} %bitcast.49, ...), kind=kLoop, calls=%fused_computation.14 | loop fusion | flops 11167744 | bytes 23969876 | tf_op jit(solution)/shard_map/add | solution.py:49
  46.7 19.5 %fusion.25 = f32[512,512]{1,0:T(8,128)} fusion(f32[512,532]{1,0:T(8,128)S(1)} %multiply_add_fusion.1, f32[]{:T(128)} %bitcast.57, f32[]{:T(128)} %bitcast.56, f32[]{:T(128)} %bitcast.55, f32[]{:T(128)} %bitcast.54, f32[]{:T(128)} %bitcast.53, f32[]{:T(128)} %bitcast.52, f32[]{:T(128)} %bitcast.51, f32[]{:T(128)} %bitcast.50, f32[]{:T(128)} %bitcast.49, ...), kind=kLoop, calls=%fused_computation.58 | loop fusion | flops 10747904 | bytes 23068756 | tf_op jit(solution)/shard_map/add | solution.py:52
  69.1 16.5 %multiply_add_fusion = f32[512,532]{1,0:T(8,128)S(1)} fusion(f32[532,532]{1,0:T(8,128)S(1)} %pad_maximum_fusion.2, f32[]{:T(128)} %bitcast.81, f32[]{:T(128)} %bitcast.80, f32[]{:T(128)} %bitcast.79, f32[]{:T(128)} %bitcast.78, f32[]{:T(128)} %bitcast.77, f32[]{:T(128)} %bitcast.76, f32[]{:T(128)} %bitcast.75, f32[]{:T(128)} %bitcast.74, f32[]{:T(128)} %bitcast.73, ...), kind=kLoop, calls=%fused_computation.13 | loop fusion | flops 11167744 | bytes 23969876 | tf_op jit(solution)/shard_map/add | solution.py:49
  85.5 19.5 %fusion.5 = f32[512,512]{1,0:T(8,128)} fusion(f32[512,532]{1,0:T(8,128)S(1)} %multiply_add_fusion, f32[]{:T(128)} %bitcast.81, f32[]{:T(128)} %bitcast.80, f32[]{:T(128)} %bitcast.79, f32[]{:T(128)} %bitcast.78, f32[]{:T(128)} %bitcast.77, f32[]{:T(128)} %bitcast.76, f32[]{:T(128)} %bitcast.75, f32[]{:T(128)} %bitcast.74, f32[]{:T(128)} %bitcast.73, ...), kind=kLoop, calls=%fused_computation.17 | loop fusion | flops 10747904 | bytes 23068756 | tf_op jit(solution)/shard_map/add | solution.py:52
  107.7 16.4 %multiply_add_fusion.2 = f32[512,532]{1,0:T(8,128)S(1)} fusion(f32[532,532]{1,0:T(8,128)S(1)} %pad_maximum_fusion.2, f32[]{:T(128)} %bitcast.33, f32[]{:T(128)} %bitcast.32, f32[]{:T(128)} %bitcast.31, f32[]{:T(128)} %bitcast.30, f32[]{:T(128)} %bitcast.29, f32[]{:T(128)} %bitcast.28, f32[]{:T(128)} %bitcast.27, f32[]{:T(128)} %bitcast.26, f32[]{:T(128)} %bitcast.25, ...), kind=kLoop, calls=%fused_computation.15 | loop fusion | flops 11167744 | bytes 23969876 | tf_op jit(solution)/shard_map/add | solution.py:49
  124.1 19.4 %constant_dynamic-update-slice_fusion.7 = (f32[512,8192]{1,0:T(8,128)}, f32[512,512]{1,0:T(8,128)S(1)}) fusion(f32[512,532]{1,0:T(8,128)S(1)} %multiply_add_fusion.2, f32[]{:T(128)} %bitcast.33, f32[]{:T(128)} %bitcast.32, f32[]{:T(128)} %bitcast.31, f32[]{:T(128)} %bitcast.30, f32[]{:T(128)} %bitcast.29, f32[]{:T(128)} %bitcast.28, f32[]{:T(128)} %bitcast.27, ...), kind=kLoop, calls=%fused_computation.154 | loop fusion | flops 10747903 | bytes 24117332
  143.6 7.3 %collective-permute-start.4 = (f32[512,512]{1,0:T(8,128)S(1)}, f32[512,512]{1,0:T(8,128)S(1)}, u32[]{:S(2)}, u32[]{:S(2)}) collective-permute-start(f32[512,512]{1,0:T(8,128)S(1)} %get-tuple-element.7), channel_id=1, source_target_pairs={{0,7},{1,0},{2,1},{3,2},{4,3},{5,4},{6,5},{7,6},{8,15},{9,8},{10,9... | collective-permute-start | bytes 3145736 | tf_op jit(solution)/shard_map/ppermute | solution.py:16
  150.8 40.0 %collective-permute-done.4 = f32[512,512]{1,0:T(8,128)S(1)} collective-permute-done((f32[512,512]{1,0:T(8,128)S(1)}, f32[512,512]{1,0:T(8,128)S(1)}, u32[]{:S(2)}, u32[]{:S(2)}) %collective-permute-start.4) | collective-permute-done | bytes 1048608 | tf_op jit(solution)/shard_map/ppermute | solution.py:16
  190.9 1.6 pad_maximum_fusion.1
  192.5 4.7 collective-permute-start.5
  200.1 58.9 %collective-permute-done.5 = f32[512,1024]{1,0:T(8,128)} collective-permute-done((f32[512,1024]{1,0:T(8,128)}, f32[512,1024]{1,0:T(8,128)}, u32[]{:S(2)}, u32[]{:S(2)}) %collective-permute-start.5) | collective-permute-done | bytes 2097184 | tf_op jit(solution)/shard_map/ppermute | solution.py:16
  259.0 4.3 pad_maximum_fusion
  263.3 2.6 collective-permute-start.6
  266.0 7.4 %copy.23 = bf16[1,512,4096]{1,2,0:T(8,128)(2,1)} copy(f32[1,512,4096]{2,1,0:T(8,128)} %param.9) | data formatting | bytes 12582912 | tf_op args[0]
  273.4 6.6 %copy.24 = bf16[512,32,128]{2,0,1:T(8,128)(2,1)} copy(bf16[512,32,128]{0,2,1:T(8,128)(2,1)} %bitcast.108) | data formatting | bytes 8388608 | tf_op jit(solution)/shard_map/convert_element_type | solution.py:60
  280.0 5.3 gather_fusion.1
  285.3 5.2 gather_fusion
  290.6 5.3 select_bitcast_fusion
  295.8 8.5 %fusion = f32[32,512,128]{1,2,0:T(8,128)} fusion(bf16[512,32,128]{2,0,1:T(8,128)(2,1)S(1)} %get-tuple-element.89, bf16[512,32,128]{2,0,1:T(8,128)(2,1)} %get-tuple-element.90, bf16[1,32,256,128]{3,2,1,0:T(8,128)(2,1)S(1)} %copy-done), kind=kOutput, calls=%fused_computation.2 | convolution fusion | flops 1090519040 | bytes 18874368 | tf_op jit(solution)/shard_map/rjk,jkn->rjn/dot_general | solution.py:64
  304.4 8.9 %copy.29 = f32[512,4096]{1,0:T(8,128)} copy(f32[512,4096]{0,1:T(8,128)} %bitcast.107) | data formatting | bytes 16777216 | tf_op jit(solution)/shard_map/reshape | solution.py:65
  313.5 2.3 constant_dynamic-update-slice_fusion.6
  315.8 3.2 constant_dynamic-update-slice_fusion.5
  319.0 229.5 %collective-permute-done.6 = f32[512,2048]{1,0:T(8,128)} collective-permute-done((f32[512,2048]{1,0:T(8,128)}, f32[512,2048]{1,0:T(8,128)}, u32[]{:S(2)}, u32[]{:S(2)}) %collective-permute-start.6) | collective-permute-done | bytes 4194336 | tf_op jit(solution)/shard_map/ppermute | solution.py:16
  548.4 4.6 constant_dynamic-update-slice_fusion.4
  555.7 3.2 constant_dynamic-update-slice_fusion.1
  558.9 4.7 constant_dynamic-update-slice_fusion
  563.6 16.6 %multiply_bitcast_fusion = f32[1,512,4096]{2,1,0:T(8,128)} fusion(f32[512,4096]{1,0:T(8,128)} %copy.29, f32[512,4096]{1,0:T(8,128)} %all-gather.5.cloned.1.call-done, f32[512,4096]{1,0:T(8,128)} %all-gather.3.cloned.1.call-done, f32[512,8192]{1,0:T(8,128)} %constant_dynamic-update-slice_fusion, s32[]{:T(128)S(6)} %select_n.53, f32[4096]{0:T(1024)S(1)} %bitcast.112, ...), kind=kLoop, calls=%fused_computation.6 | loop fusion | flops 27262976 | bytes 42059780 | tf_op jit(solution)/shard_map/broadcast_in_dim | solution.py:104
  (56 shorter events, 19.1 us)
Async XLA Ops:
  6.5 289.3 %copy-start = (bf16[1,32,256,128]{3,2,1,0:T(8,128)(2,1)S(1)}, bf16[1,32,256,128]{3,2,1,0:T(8,128)(2,1)}, u32[]{:S(2)}) copy-start(bf16[1,32,256,128]{3,2,1,0:T(8,128)(2,1)} %param.10) | copy-start | bytes 6291460
  6.5 557.1 %all-gather.3.cloned.1.call-start = ((), (), s32[]{:S(2)}) async-start(), calls=%async_computation | async-start | bytes 9437184 | tf_op jit(solution)/shard_map/all_gather | solution.py:84
  6.5 23.2 %copy-start.3 = (f32[512,512]{1,0:T(8,128)S(1)}, f32[512,512]{1,0:T(8,128)}, u32[]{:S(2)}) copy-start(f32[512,512]{1,0:T(8,128)} %param.12) | copy-start | bytes 3145732
  7.5 5.8 collective-permute-start
  10.0 5.2 collective-permute-start.1
  16.4 8.6 %collective-permute-start.2 = (f32[532,10]{1,0:T(8,128)S(1)}, f32[532,10]{1,0:T(8,128)S(1)}, u32[]{:S(2)}, u32[]{:S(2)}) collective-permute-start(f32[532,10]{1,0:T(8,128)S(1)} %get-tuple-element.10), channel_id=1, source_target_pairs={{0,1},{1,2},{2,3},{3,4},{4,5},{5,6},{6,7},{8,9},{9,10},{10,11},{11... | collective-permute-start | bytes 63848 | tf_op jit(solution)/shard_map/ppermute | solution.py:30
  19.8 9.9 %collective-permute-start.3 = (f32[532,10]{1,0:T(8,128)S(1)}, f32[532,10]{1,0:T(8,128)S(1)}, u32[]{:S(2)}, u32[]{:S(2)}) collective-permute-start(f32[532,10]{1,0:T(8,128)S(1)} %get-tuple-element.11), channel_id=1, source_target_pairs={{1,0},{2,1},{3,2},{4,3},{5,4},{6,5},{7,6},{9,8},{10,9},{11,10},{12... | collective-permute-start | bytes 63848 | tf_op jit(solution)/shard_map/ppermute | solution.py:31
  66.2 497.4 %all-gather.5.cloned.1.call-start = ((), (), s32[]{:S(2)}) async-start(), calls=%async_computation.1 | async-start | bytes 9437184 | tf_op jit(solution)/shard_map/all_gather | solution.py:85
  143.6 53.7 %copy-start.4 = (f32[8,4,3,3]{0,1,3,2:T(4,128)S(1)}, f32[8,4,3,3]{0,1,3,2:T(4,128)}, u32[]{:S(2)}) copy-start(f32[8,4,3,3]{0,1,3,2:T(4,128)} %param.13) | copy-start | bytes 3460
  143.6 47.3 %collective-permute-start.4 = (f32[512,512]{1,0:T(8,128)S(1)}, f32[512,512]{1,0:T(8,128)S(1)}, u32[]{:S(2)}, u32[]{:S(2)}) collective-permute-start(f32[512,512]{1,0:T(8,128)S(1)} %get-tuple-element.7), channel_id=1, source_target_pairs={{0,7},{1,0},{2,1},{3,2},{4,3},{5,4},{6,5},{7,6},{8,15},{9,8},{10,9... | collective-permute-start | bytes 3145736 | tf_op jit(solution)/shard_map/ppermute | solution.py:16
  190.9 1.7 copy-start.1
  192.5 66.5 %collective-permute-start.5 = (f32[512,1024]{1,0:T(8,128)}, f32[512,1024]{1,0:T(8,128)}, u32[]{:S(2)}, u32[]{:S(2)}) collective-permute-start(f32[512,1024]{1,0:T(8,128)} %pad_maximum_fusion.1), channel_id=1, source_target_pairs={{0,6},{1,7},{2,0},{3,1},{4,2},{5,3},{6,4},{7,5},{8,14},{9,15},{10,... | collective-permute-start | bytes 6291464 | tf_op jit(solution)/shard_map/ppermute | solution.py:16
  263.3 285.1 %collective-permute-start.6 = (f32[512,2048]{1,0:T(8,128)}, f32[512,2048]{1,0:T(8,128)}, u32[]{:S(2)}, u32[]{:S(2)}) collective-permute-start(f32[512,2048]{1,0:T(8,128)} %pad_maximum_fusion), channel_id=1, source_target_pairs={{0,4},{1,5},{2,6},{3,7},{4,0},{5,1},{6,2},{7,3},{8,12},{9,13},{10,... | collective-permute-start | bytes 12582920 | tf_op jit(solution)/shard_map/ppermute | solution.py:16
  273.4 6.6 %copy-start.5 = (s32[1,32]{1,0:T(1,128)S(1)}, s32[1,32]{1,0:T(1,128)}, u32[]{:S(2)}) copy-start(s32[1,32]{1,0:T(1,128)} %param.11) | copy-start | bytes 388
  553.0 1.6 copy-start.2
Sparse Core Ops, SparseCore 0:
  66.3 162.6 all-gather.2
  231.3 286.1 all-gather.4
